TPU v7x, 1024 devices: a whole 8x8x8 slice. The times are simulated.
1024 devices in a mesh: wave: 64 (over z, y), lev: 16 (over x, core).
Axes of the slice: x: 8, y: 8, z: 8, core: 2. Of those that a mesh axis runs over, the one named last changes fastest.
Arguments:
- spectra: bfloat16 [640, 3, 96, 2, 640], P('wave', None, 'lev'), may hold values from -0.3125 to 0.3125
- vertical: bfloat16 [3, 96, 96], replicated, may hold values from -0.625 to 0.625
- legendre: bfloat16 [640, 64, 640], P('wave'), may hold values from -0.25 to 0.25
- tile_mask: int32 [640, 10, 1], P('wave'), may hold values from 0 to 1, as said below
- assign: int32 [640], replicated, may hold values from 0 to 639, as said below
- row_points: int32 [64], P('wave'), may hold values from 20 to 2576, as said below
- quadrature: float32 [64], P('wave'), may hold values from 10 to 100
- forcing: bfloat16 [3, 96, 2, 64, 2688], P(None, 'lev', None, 'wave'), may hold values from -6 to 6
Outputs:
- grid_field: bfloat16 [3, 96, 2, 64, 2688], P(None, 'lev', None, 'wave')
- spectra_out: bfloat16 [640, 3, 96, 2, 640], P('wave', None, 'lev')
Inputs may be any that keep to these rules, and one draw needn't show every extreme that they name: `assign`: every zonal wavenumber is held by exactly one slot; the slots of one wave index are consecutive. tile_mask[s, b, r] = 1 marks a nonzero Legendre tile of slot s: total wavenumbers b * 64 to (b + 1) * 64 - 1, north rows r * 64 to (r + 1) * 64 - 1. A tile is marked only if it holds some total wavenumber at or above the slot's zonal wavenumber. row_points[h] = 20 + 4 i, with i the octahedral index of north row h counted from the pole; i rises strictly with h, and the last north row is the one next to the equator, with 2576 points.
All inputs are finite; a program needn't handle non-finite values.
Results may differ from a plain program's by a relative error of at most 0.0085.
Values may be sent and summed in bfloat16 or wider, within the bound.
A program may use at most 64 MiB of HBM per device.

v0:
```python
import math

import jax
import jax.numpy as jnp
from jax import lax
from jax.sharding import PartitionSpec as P


def phase_table(wave_numbers, row_length, point_count):
    wave_count = wave_numbers.shape[0]
    column = lax.broadcasted_iota(jnp.int32, (wave_count, point_count), 1)
    remainder = wave_numbers[:, None] * column % row_length
    angles = remainder.astype(jnp.float32) * (2.0 * math.pi / row_length.astype(jnp.float32))
    usable = (column < row_length) & (2 * wave_numbers[:, None] < row_length)
    cosine = jnp.where(usable, jnp.cos(angles), jnp.float32(0.0)).astype(jnp.bfloat16)
    minus_sine = jnp.where(usable, -jnp.sin(angles), jnp.float32(0.0)).astype(jnp.bfloat16)
    return jnp.concatenate([cosine, minus_sine], 0)


def row_dense(channel_rows, forcing_row, wave_numbers, row_length, row_scale):
    store_width = forcing_row.shape[1]
    phase_rows = phase_table(wave_numbers, row_length, store_width)
    grid_row = jnp.dot(channel_rows, phase_rows, preferred_element_type=jnp.float32).astype(
        jnp.bfloat16
    )
    summed = (grid_row.astype(jnp.float32) + forcing_row.astype(jnp.float32)).astype(jnp.bfloat16)
    fourier_back = lax.dot_general(
        summed, phase_rows, (((1,), (1,)), ((), ())), preferred_element_type=jnp.float32
    )
    return (grid_row, (fourier_back * row_scale).astype(jnp.bfloat16))


def body(spectra, vertical, legendre, tile_mask, assign, row_points, quadrature, forcing):
    slot_count = spectra.shape[0]
    level_count = spectra.shape[2]
    degrees = spectra.shape[4]
    wave_rank = lax.axis_index("wave")
    own_waves = lax.dynamic_slice_in_dim(assign, wave_rank * slot_count, slot_count)
    own_rows = lax.dynamic_slice_in_dim(
        vertical, lax.axis_index("lev") * level_count, level_count, 1
    )
    coupled = jnp.einsum(
        "fab,sfbrn->sfarn",
        own_rows,
        lax.all_gather(spectra, "lev", axis=2, tiled=True),
        preferred_element_type=jnp.float32,
    ).astype(jnp.bfloat16)
    tile_height = degrees // tile_mask.shape[1]
    tile_span = legendre.shape[1] // tile_mask.shape[2]
    blocked = legendre.reshape(
        slot_count, tile_mask.shape[2], tile_span, tile_mask.shape[1], tile_height
    )
    mask_rows = jnp.transpose(tile_mask, (0, 2, 1))
    live_table = jnp.where(
        mask_rows[:, :, None, :, None] > 0, blocked, jnp.zeros_like(blocked)
    ).reshape(legendre.shape)
    degree_index = lax.broadcasted_iota(jnp.int32, (slot_count, degrees), 1)
    offset = degree_index - own_waves[:, None]
    south_sign = jnp.where(offset % 2 == 0, 1.0, -1.0)
    present = offset >= 0
    both_signs = jnp.stack([jnp.ones_like(south_sign), south_sign], 1)
    signs = jnp.where(present[:, None, :], both_signs, 0.0).astype(jnp.bfloat16)
    signed = coupled[:, :, :, None, :, :] * signs[:, None, None, :, None, :]
    fourier = jnp.einsum(
        "sfaern,shn->hfaers", signed, live_table, preferred_element_type=jnp.float32
    ).astype(jnp.bfloat16)
    by_rows = lax.all_to_all(fourier, "wave", split_axis=0, concat_axis=5, tiled=True)
    factors = jnp.where(assign == 0, 1.0, 2.0).astype(jnp.bfloat16)
    channels = by_rows.shape[1] * by_rows.shape[2] * 2
    channel_rows = (by_rows[0] * factors).reshape(channels, 2 * assign.shape[0])
    forcing_row = forcing[:, :, :, 0, :].reshape(channels, forcing.shape[4])
    row_length = row_points[0]
    row_scale = quadrature[0] / row_length.astype(jnp.float32)
    grid_row, weighted = row_dense(channel_rows, forcing_row, assign, row_length, row_scale)
    grid_rows = [grid_row.reshape(forcing.shape[0], forcing.shape[1], 2, forcing.shape[4])]
    weighted_rows = [weighted.reshape(by_rows.shape[1:])]
    grid_field = jnp.stack(grid_rows, 3)
    weighted_all = jnp.stack(weighted_rows, 0)
    by_slots = lax.all_to_all(weighted_all, "wave", split_axis=5, concat_axis=0, tiled=True)
    projected = jnp.einsum(
        "hfaers,shn->sfaern", by_slots, live_table, preferred_element_type=jnp.float32
    )
    combined = jnp.sum(projected * signs[:, None, None, :, None, :].astype(jnp.float32), axis=3)
    return (grid_field, combined.astype(jnp.bfloat16))


def solution(mesh):
    return jax.shard_map(
        body,
        mesh=mesh,
        in_specs=(
            P("wave", None, "lev", None, None),
            P(),
            P("wave", None, None),
            P("wave", None, None),
            P(),
            P("wave"),
            P("wave"),
            P(None, "lev", None, "wave", None),
        ),
        out_specs=(P(None, "lev", None, "wave", None), P("wave", None, "lev", None, None)),
        check_vma=False,
    )
```

profile of v0, /device:TPU:1, one launch (start us, length us, event | category | flops | bytes accessed | tf_op | source)
XLA Modules:
  0.0 197.7 jit_solution(973191612181804231)
XLA Ops:
  7.2 2.1 %copy.26 = bf16[10,3,6,2,640]{4,3,1,0,2:T(2,128)(2,1)} copy(bf16[10,3,6,2,640]{4,3,2,1,0:T(2,128)(2,1)} %param.8) | data formatting | bytes 921600 | tf_op args[0]
  10.7 0.7 fusion.39
  11.6 0.8 dynamic_slice.7
  12.4 0.7 multiply_compare_fusion
  13.4 95.6 %fusion.2 = (bf16[640,2688]{1,0:T(8,128)(2,1)}, bf16[640,2688]{1,0:T(8,128)(2,1)}) fusion(f32[]{:T(128)S(6)} %div.6, s32[]{:T(128)S(6)} %select_n.68, s32[640]{0:T(1024)} %param.12, pred[]{:T(512)S(6)} %lt.42, pred[2688]{0:T(1024)(128)(4,1)S(1)} %iota_compare_fusion, pred[640]{0:T(1024)(128)(4,1)S(1)} %multiply_compare_fusion), kind=kLoop, calls=%fused_computation.5 | loop fusion | flops 27525120 | bytes 6887177 | tf_op jit(solution)/shard_map/convert_element_type | solution.py:15
  109.1 4.2 %fusion.18 = bf16[10,3,6,2,640]{4,2,3,1,0:T(8,128)(2,1)S(1)} fusion(bf16[10,3,96,2,640]{4,3,1,0,2:T(2,128)(2,1)} %all-gather.2.cloned.1.call-done, bf16[3,96,96]{2,1,0:T(8,128)(2,1)S(1)} %copy-done, s32[]{:T(128)S(6)} %select_n.62), kind=kOutput, calls=%fused_computation.22 | convolution fusion | flops 44467200 | bytes 7839748 | tf_op jit(solution)/shard_map/fab,sfbrn->sfarn/dot_general | solution.py:42
  113.8 2.0 %copy.28 = bf16[64,3,6,2,2,10]{5,4,3,2,1,0:T(2,128)(2,1)S(1)} copy(bf16[64,3,6,2,2,10]{0,2,4,3,1,5:T(8,128)(2,1)S(1)} %fusion.26) | data formatting | bytes 184320 | tf_op jit(solution)/shard_map/convert_element_type | solution.py:66
  115.8 2.0 reshape.115
  117.8 24.1 %all-to-all-start = ((bf16[64,2,360]{2,1,0:T(2,128)(2,1)}), bf16[64,2,360]{2,1,0:T(2,128)(2,1)S(1)}, u32[]{:S(2)}, u32[]{:S(2)}) async-start(bf16[64,2,360]{2,1,0:T(2,128)(2,1)} %reshape.115), calls=%async_computation | async-start | bytes 196608 | tf_op jit(solution)/shard_map/all_to_all | solution.py:67
  142.3 10.9 %all-to-all-done = bf16[64,2,360]{2,1,0:T(2,128)(2,1)S(1)} async-done(((bf16[64,2,360]{2,1,0:T(2,128)(2,1)}), bf16[64,2,360]{2,1,0:T(2,128)(2,1)S(1)}, u32[]{:S(2)}, u32[]{:S(2)}) %all-to-all-start) | async-done | bytes 92192 | tf_op jit(solution)/shard_map/all_to_all | solution.py:67
  153.1 0.6 reshape.116
  154.1 2.1 %squeeze.9 = bf16[36,1280]{1,0:T(8,128)(2,1)S(1)} reshape(bf16[1,3,6,2,2,64,10]{6,5,4,3,2,1,0:T(8,128)(2,1)S(1)} %copy.29) | data formatting | bytes 184320 | tf_op jit(solution)/shard_map/squeeze | solution.py:70
  156.2 4.5 %fusion.12 = bf16[36,2688]{1,0:T(8,128)(2,1)S(1)} fusion(bf16[640,2688]{1,0:T(8,128)(2,1)} %get-tuple-element.13, bf16[640,2688]{1,0:T(8,128)(2,1)} %get-tuple-element.12, bf16[36,1280]{1,0:T(8,128)(2,1)S(1)} %squeeze.9, bf16[1280]{0:T(1024)(128)(2,1)S(1)} %mul.73), kind=kOutput, calls=%fused_computation.17 | convolution fusion | flops 261631488 | bytes 7169536 | tf_op jit(solution)/shard_map/dot_general | solution.py:23
  160.6 0.5 copy-done.2
  161.2 2.2 %fusion.14 = bf16[36,1280]{1,0:T(8,128)(2,1)S(1)} fusion(bf16[640,2688]{1,0:T(8,128)(2,1)S(1)} %copy-done.2, bf16[640,2688]{1,0:T(8,128)(2,1)S(1)} %copy-done.1, f32[36,2688]{1,0:T(8,128)S(1)} %reshape.112, bf16[36,2688]{1,0:T(8,128)(2,1)S(1)} %fusion.12, f32[]{:T(128)S(6)} %div.7), kind=kOutput, calls=%fused_computation.20 | convolution fusion | flops 261871104 | bytes 7554052 | tf_op jit(solution)/shard_map/dot_general | solution.py:27
  163.5 2.7 %copy.30 = bf16[1,3,6,2,2,640]{2,4,3,1,0,5:T(2,128)(2,1)S(1)} copy(bf16[1,3,6,2,2,640]{5,4,3,2,1,0:T(2,128)(2,1)S(1)} %stack_reshape.7) | data formatting | bytes 184320 | tf_op jit(solution)/shard_map/stack;reshape | solution.py:78
  166.1 2.7 %reshape.117 = bf16[64,2,360]{2,1,0:T(2,128)(2,1)} reshape(bf16[640,1,3,2,2,6]{5,4,3,2,1,0:T(2,128)(2,1)S(1)} %bitcast.42) | data formatting | bytes 184320
  168.9 4.6 %all-to-all-start.1 = ((bf16[64,2,360]{2,1,0:T(2,128)(2,1)}), bf16[64,2,360]{2,1,0:T(2,128)(2,1)S(1)}, u32[]{:S(2)}, u32[]{:S(2)}) async-start(bf16[64,2,360]{2,1,0:T(2,128)(2,1)} %reshape.117), calls=%async_computation.1 | async-start | bytes 196608 | tf_op jit(solution)/shard_map/all_to_all | solution.py:79
  173.5 0.9 stack_reshape.6
  174.4 10.4 %all-to-all-done.1 = bf16[64,2,360]{2,1,0:T(2,128)(2,1)S(1)} async-done(((bf16[64,2,360]{2,1,0:T(2,128)(2,1)}), bf16[64,2,360]{2,1,0:T(2,128)(2,1)S(1)}, u32[]{:S(2)}, u32[]{:S(2)}) %all-to-all-start.1) | async-done | bytes 92192 | tf_op jit(solution)/shard_map/all_to_all | solution.py:79
  184.8 1.1 reshape.118
  185.9 2.1 %copy.32 = bf16[1,3,6,2,2,64,10]{5,2,4,3,1,6,0:T(8,128)(2,1)S(1)} copy(bf16[1,3,6,2,2,64,10]{2,4,3,1,6,5,0:T(2,128)(2,1)S(1)} %bitcast.43) | data formatting | bytes 184320 | tf_op jit(solution)/shard_map/all_to_all | solution.py:79
  188.0 1.8 multiply_reduce_fusion
  189.8 1.1 copy.34
  (27 shorter events, 1.8 us)
Async XLA Ops:
  7.2 101.9 %copy-start = (bf16[3,96,96]{2,1,0:T(8,128)(2,1)S(1)}, bf16[3,96,96]{2,1,0:T(8,128)(2,1)}, u32[]{:S(2)}) copy-start(bf16[3,96,96]{2,1,0:T(8,128)(2,1)} %param.9) | copy-start | bytes 165892
  7.2 101.9 %all-gather.2.cloned.1.call-start = ((), (), s32[]{:S(2)}) async-start(), calls=%async_computation.2 | async-start | bytes 7833600 | tf_op jit(solution)/shard_map/all_gather | solution.py:45
  13.4 99.9 %copy-start.5 = (bf16[10,64,640]{2,1,0:T(8,128)(2,1)S(1)}, bf16[10,64,640]{2,1,0:T(8,128)(2,1)}, u32[]{:S(2)}) copy-start(bf16[10,64,640]{2,1,0:T(8,128)(2,1)} %param.10) | copy-start | bytes 2457604
  109.0 32.9 %copy-start.4 = (s32[640]{0:T(1024)S(1)}, s32[640]{0:T(1024)}, u32[]{:S(2)}) copy-start(s32[640]{0:T(1024)} %param.12) | copy-start | bytes 7684
  109.0 32.9 %copy-start.3 = (bf16[3,6,2,1,2688]{4,2,3,1,0:T(2,128)(2,1)S(1)}, bf16[3,6,2,1,2688]{4,2,3,1,0:T(2,128)(2,1)}, u32[]{:S(2)}) copy-start(bf16[3,6,2,1,2688]{4,2,3,1,0:T(2,128)(2,1)} %param.15) | copy-start | bytes 580612
  117.8 35.4 %all-to-all-start = ((bf16[64,2,360]{2,1,0:T(2,128)(2,1)}), bf16[64,2,360]{2,1,0:T(2,128)(2,1)S(1)}, u32[]{:S(2)}, u32[]{:S(2)}) async-start(bf16[64,2,360]{2,1,0:T(2,128)(2,1)} %reshape.115), calls=%async_computation | async-start | bytes 196608 | tf_op jit(solution)/shard_map/all_to_all | solution.py:67
  156.2 4.5 %copy-start.1 = (bf16[640,2688]{1,0:T(8,128)(2,1)S(1)}, bf16[640,2688]{1,0:T(8,128)(2,1)}, u32[]{:S(2)}) copy-start(bf16[640,2688]{1,0:T(8,128)(2,1)} %get-tuple-element.12) | copy-start | bytes 10321924
  156.2 5.0 %copy-start.2 = (bf16[640,2688]{1,0:T(8,128)(2,1)S(1)}, bf16[640,2688]{1,0:T(8,128)(2,1)}, u32[]{:S(2)}) copy-start(bf16[640,2688]{1,0:T(8,128)(2,1)} %get-tuple-element.13) | copy-start | bytes 10321924
  168.9 15.9 %all-to-all-start.1 = ((bf16[64,2,360]{2,1,0:T(2,128)(2,1)}), bf16[64,2,360]{2,1,0:T(2,128)(2,1)S(1)}, u32[]{:S(2)}, u32[]{:S(2)}) async-start(bf16[64,2,360]{2,1,0:T(2,128)(2,1)} %reshape.117), calls=%async_computation.1 | async-start | bytes 196608 | tf_op jit(solution)/shard_map/all_to_all | solution.py:79
Sparse Core Ops, SparseCore 0:
  11.3 68.7 all-gather.1
where the time goes:
time: 200 us; the launch traced here: 198 us
  other arithmetic  97.3 us (49%)
  starting transfers between devices  28.8 us (14%)
  local copies, waits for them, and re-layouts  21.5 us (11%)
  waiting for transfers between devices  21.3 us (11%)
  between operations  15.7 us (8%)
  matrix products  13.1 us (7%)
    convert_element_type x1, other arithmetic, phase_table(): jnp.where(usable, jnp.cos(angles), jnp.float32(0.0)).astype(jnp.bfloat16)  95.6 us
    all_to_all x1, starting transfers between devices, body(): lax.all_to_all(fourier, 'wave', split_axis=0, concat_axis=5, tiled=True)  24.1 us
    all_to_all x1, waiting for transfers between devices, body(): lax.all_to_all(fourier, 'wave', split_axis=0, concat_axis=5, tiled=True)  10.9 us
    all_to_all x1, waiting for transfers between devices, body(): lax.all_to_all(weighted_all, 'wave', split_axis=5, concat_axis=0, tiled=T...  10.4 us
    unnamed x18, local copies, waits for them, and re-layouts  10.2 us
    all_to_all x1, starting transfers between devices, body(): lax.all_to_all(weighted_all, 'wave', split_axis=5, concat_axis=0, tiled=T...  4.62 us
    dot_general x1, matrix products, row_dense(): jnp.dot(channel_rows, phase_rows, preferred_element_type=jnp.float32)  4.46 us
    dot_general x1, matrix products, body(): jnp.einsum('fab,sfbrn->sfarn', own_rows, lax.all_gather(spectra, 'lev', a...  4.21 us
  transfers between devices with their start and end apart: 3, of which 2 were waited for; matrix products, arithmetic and copies ran while one was open for 50% of the time, Pallas kernels for 0%

commit v1 on v0

v1 whole, which is shorter than its diff:
```python
import functools
import math

import jax
import jax.numpy as jnp
from jax import lax
from jax.experimental import pallas as pl
from jax.experimental.pallas import tpu as pltpu
from jax.sharding import PartitionSpec as P

MESH = pl.DeviceIdType.MESH
F32 = jnp.float32
BF16 = jnp.bfloat16
LANES = 128
FIELDS = 3
OWN_LEVELS = 6
SLOTS = 10
GROUPS = 4
THIRDS = 3
PITCH = 40
LEVEL_PITCH = 24
ROWS = 2 * GROUPS
CHANNELS = 2 * FIELDS * OWN_LEVELS
NT_DIMS = (((1,), (1,)), ((), ()))


def cosine_of_turns(turns):
    angle = (turns - jnp.round(turns)) * F32(2.0 * math.pi)
    square = angle * angle
    total = jnp.full_like(square, (-1.0) ** 9 / math.factorial(18))
    for k in range(8, -1, -1):
        total = total * square + F32((-1.0) ** k / math.factorial(2 * k))
    return total


def turns_of(product, length, inverse):
    return (product - jnp.floor(product * inverse) * length) * inverse


def slots_of():
    return [(s, s // GROUPS, s % GROUPS) for s in range(SLOTS)]


def kernel(
    waves,
    levs,
    spectra,
    legendre,
    tiles,
    assign,
    row_points,
    quadrature,
    vertical,
    forcing,
    grid_out,
    spectra_out,
    weights,
    mixer,
    phase,
    plane,
    rows32,
    turned,
    spread,
    channels,
    summed,
    send_a,
    recv_a,
    send_b,
    recv_b,
    send_c,
    recv_c,
    send_sems,
    recv_sems,
):
    wave = lax.axis_index("wave")
    lev = lax.axis_index("lev")
    own_rows = waves // levs
    part = own_rows * ROWS
    total_rows = waves * ROWS
    degrees = spectra.shape[2]
    points = forcing.shape[1]

    barrier = pltpu.get_barrier_semaphore()

    def greet_lev(k, carry):
        pl.semaphore_signal(
            barrier, inc=1, device_id=(wave, lax.rem(lev + k, levs)), device_id_type=MESH
        )
        return carry

    def greet_wave(k, carry):
        pl.semaphore_signal(
            barrier, inc=1, device_id=(lax.rem(wave + k, waves), lev), device_id_type=MESH
        )
        return carry

    lax.fori_loop(1, levs, greet_lev, 0)
    lax.fori_loop(1, waves, greet_wave, 0)

    turned[...] = jnp.zeros_like(turned)
    plane[...] = jnp.zeros_like(plane)
    degree = lax.broadcasted_iota(jnp.int32, (1, degrees), 1)
    lane = lax.broadcasted_iota(jnp.int32, (1, LANES), 1)
    half = degrees // (2 * LANES // 2)
    for s, third, group in slots_of():
        wave_number = assign[wave * SLOTS + s]
        marks = jnp.concatenate(
            [
                jnp.where(lane < LANES // 2, tiles[s, 2 * k], tiles[s, 2 * k + 1])
                for k in range(half)
            ],
            axis=1,
        )
        offset = degree - wave_number
        live = jnp.where((marks > 0) & (offset >= 0), F32(1.0), F32(0.0))
        signed = jnp.where((offset & 1) == 0, live, -live)
        table = legendre[s].astype(F32)
        lath = table.shape[0]
        weights[s, 0:lath, :] = (table * live).astype(BF16)
        weights[s, lath : 2 * lath, :] = (table * signed).astype(BF16)
        factor = jnp.where(wave_number == 0, F32(1.0), F32(2.0))
        plane[0:CHANNELS, 0 : 2 * lath] = factor * lax.dot_general(
            spectra[s], weights[s], NT_DIMS, preferred_element_type=F32
        )
        for part_at in range(2):
            block = plane[pl.ds(part_at, PITCH // 2, stride=2), :]
            row = group * 2 + part_at
            base = row * LANES + third * PITCH
            turned[pl.ds(base, PITCH // 2, stride=2), :] = block
            turned[pl.ds(base + 1, PITCH // 2, stride=2), :] = pltpu.roll(
                block, LANES - lath, axis=1
            )
    for row in range(ROWS):
        flipped = turned[row * LANES : (row + 1) * LANES, :].T
        spread[pl.ds(row, waves, stride=ROWS), :] = flipped[0:waves, :]
    send_a[...] = spread[0:total_rows, :].astype(BF16)

    pl.semaphore_wait(barrier, levs - 1 + waves - 1)

    def copy_a(target):
        return pltpu.make_async_remote_copy(
            src_ref=send_a.at[pl.ds(pl.multiple_of(target * part, part), part), :],
            dst_ref=recv_a.at[lev],
            send_sem=send_sems.at[0],
            recv_sem=recv_sems.at[0],
            device_id=(wave, target),
            device_id_type=MESH,
        )

    def start_a(k, carry):
        copy_a(lax.rem(lev + k, levs)).start()
        return carry

    lax.fori_loop(1, levs, start_a, 0)
    own_a = pltpu.make_async_copy(
        send_a.at[pl.ds(pl.multiple_of(lev * part, part), part), :],
        recv_a.at[lev],
        recv_sems.at[0],
    )
    own_a.start()

    levels = vertical.shape[1]
    edge = levs * LEVEL_PITCH
    at_row = lax.broadcasted_iota(jnp.int32, (edge, levels), 0)
    at_level = lax.broadcasted_iota(jnp.int32, (edge, levels), 1)
    at_group = (at_row * 2731) >> 16
    at_inner = at_row - at_group * LEVEL_PITCH
    at_field = (at_inner * 43) >> 8
    wanted = at_group * OWN_LEVELS + at_inner - at_field * OWN_LEVELS
    mixed = jnp.zeros((edge, edge), F32)
    for field in range(FIELDS):
        pick = jnp.where((at_field == field) & (at_level == wanted), F32(1.0), F32(0.0)).astype(
            BF16
        )
        rows = jnp.dot(pick, vertical[field], preferred_element_type=F32).astype(BF16)
        mixed = mixed + lax.dot_general(rows, pick, NT_DIMS, preferred_element_type=F32)
    mixer[...] = mixed.astype(BF16)

    length = row_points[0]
    length_f = length.astype(F32)
    inverse = F32(1.0) / length_f
    fine = THIRDS * 2 * ROWS
    at = lax.broadcasted_iota(jnp.int32, (2 * ROWS, LANES), 0)
    at_pair = at >> 1
    quarter = (at & 1).astype(F32) * F32(0.25)
    column = lax.broadcasted_iota(jnp.int32, (2 * ROWS, LANES), 1).astype(F32)

    def phase_rows(step, carry):
        numbers = []
        for third in range(THIRDS):
            number = jnp.zeros((2 * ROWS, LANES), jnp.int32)
            for pair in range(2):
                for group in range(GROUPS):
                    s = third * GROUPS + group
                    if s < SLOTS:
                        held = assign[(step * 2 + pair) * SLOTS + s]
                        number = jnp.where(at_pair == pair * GROUPS + group, held, number)
            numbers.append(number)
        number = jnp.concatenate(numbers, axis=0)
        real = [[s < SLOTS for s in range(t * GROUPS, (t + 1) * GROUPS)] for t in range(THIRDS)]
        usable = 2 * number < length
        group_at = at_pair & (GROUPS - 1)
        kept = jnp.concatenate(
            [jnp.where(group_at < sum(real[t]), F32(1.0), F32(0.0)) for t in range(THIRDS)], axis=0
        )
        kept = jnp.where(usable, kept, F32(0.0))
        number = number.astype(F32)
        columns = jnp.concatenate([column] * THIRDS, axis=0)
        quarters = jnp.concatenate([quarter] * THIRDS, axis=0)
        before = kept * cosine_of_turns(turns_of(number * columns, length_f, inverse) + quarters)
        now = kept * cosine_of_turns(
            turns_of(number * (columns + F32(LANES)), length_f, inverse) + quarters
        )
        twice = F32(2.0) * cosine_of_turns(turns_of(number * F32(LANES), length_f, inverse))
        for block in range(points // LANES):
            value = before.astype(BF16)
            for third in range(THIRDS):
                phase[
                    pl.ds(pl.multiple_of(third * total_rows + step * 2 * ROWS, 2 * ROWS), 2 * ROWS),
                    block * LANES : (block + 1) * LANES,
                ] = value[third * 2 * ROWS : (third + 1) * 2 * ROWS, :]
            before, now = now, twice * now - before
        return carry

    lax.fori_loop(0, waves // 2, phase_rows, 0)

    whole_a = pltpu.make_async_copy(recv_a, recv_a, recv_sems.at[0])
    whole_a.wait()
    for source in range(levs):
        rows32[source * LANES : (source + 1) * LANES, 0:part] = recv_a[source].astype(F32).T
    for third in range(THIRDS):
        for side in range(2):
            start = third * PITCH + side
            block = jnp.concatenate(
                [
                    rows32[pl.ds(source * LANES + start, LEVEL_PITCH, stride=2), :]
                    for source in range(levs)
                ],
                axis=0,
            ).astype(BF16)
            product = jnp.dot(mixer[...], block, preferred_element_type=F32)
            for target in range(levs):
                turned[pl.ds(target * LANES + start, PITCH // 2, stride=2), :] = product[
                    target * LEVEL_PITCH : target * LEVEL_PITCH + PITCH // 2, :
                ]
    for target in range(levs):
        flipped = turned[target * LANES : (target + 1) * LANES, :].T[0:part, :]
        send_b[target] = flipped.astype(BF16).reshape(own_rows, ROWS, LANES)

    def place_b(k):
        turn = lax.rem(k + wave + lev, waves)
        target = turn // own_rows
        row = lax.rem(turn, own_rows)
        return row, target, (lev * own_rows + row == wave) & (target == lev)

    def copy_b(row, target):
        return pltpu.make_async_remote_copy(
            src_ref=send_b.at[target, row],
            dst_ref=recv_b.at[wave],
            send_sem=send_sems.at[1],
            recv_sem=recv_sems.at[1],
            device_id=(lev * own_rows + row, target),
            device_id_type=MESH,
        )

    def start_b(k, carry):
        row, target, here = place_b(k)

        @pl.when(here)
        def _():
            pltpu.make_async_copy(send_b.at[target, row], recv_b.at[wave], recv_sems.at[1]).start()

        @pl.when(jnp.logical_not(here))
        def _():
            copy_b(row, target).start()

        return carry

    lax.fori_loop(0, waves, start_b, 0)
    pltpu.make_async_copy(recv_b, recv_b, recv_sems.at[1]).wait()

    received = recv_b[...].astype(F32).reshape(total_rows, LANES)
    for block in range(total_rows // LANES):
        flipped = received[block * LANES : (block + 1) * LANES, :].T
        for third in range(THIRDS):
            at_lane = third * total_rows + block * LANES
            channels[:, at_lane : at_lane + LANES] = flipped[
                third * PITCH : (third + 1) * PITCH, :
            ].astype(BF16)
    chunk = 3 * LANES if points % (3 * LANES) == 0 else LANES
    for first in range(0, points, chunk):
        inside = first + lax.broadcasted_iota(jnp.int32, (CHANNELS, chunk), 1) < length
        grid = jnp.dot(
            channels[0:CHANNELS, :], phase[:, first : first + chunk], preferred_element_type=F32
        )
        grid = jnp.where(inside, grid, F32(0.0)).astype(BF16)
        grid_out[:, first : first + chunk] = grid
        both = grid.astype(F32) + forcing[:, first : first + chunk].astype(F32)
        summed[:, first : first + chunk] = jnp.where(inside, both, F32(0.0)).astype(BF16)
    scale = quadrature[0] / length_f
    plane[...] = jnp.zeros_like(plane)
    for block in range(total_rows // LANES):
        for third in range(THIRDS):
            first = third * total_rows + block * LANES
            back = lax.dot_general(
                summed[...], phase[first : first + LANES, :], NT_DIMS, preferred_element_type=F32
            )
            plane[third * PITCH : third * PITCH + CHANNELS, :] = back * scale
        send_c[block * LANES // ROWS : (block + 1) * LANES // ROWS] = (
            plane[...].T.astype(BF16).reshape(LANES // ROWS, ROWS, LANES)
        )

    def copy_c(k):
        target = lax.rem(wave + k, waves)
        return pltpu.make_async_remote_copy(
            src_ref=send_c.at[target],
            dst_ref=recv_c.at[wave],
            send_sem=send_sems.at[2],
            recv_sem=recv_sems.at[2],
            device_id=(target, lev),
            device_id_type=MESH,
        )

    def start_c(k, carry):
        copy_c(k).start()
        return carry

    lax.fori_loop(1, waves, start_c, 0)
    pltpu.make_async_copy(send_c.at[wave], recv_c.at[wave], recv_sems.at[2]).start()
    pltpu.make_async_copy(recv_c, recv_c, recv_sems.at[2]).wait()

    spread[0:total_rows, :] = recv_c[...].astype(F32).reshape(total_rows, LANES)
    for row in range(ROWS):
        turned[row * LANES : (row + 1) * LANES, 0:waves] = spread[
            pl.ds(row, waves, stride=ROWS), :
        ].T
    for s, third, group in slots_of():
        for part_at in range(2):
            base = (group * 2 + part_at) * LANES + third * PITCH
            north = turned[pl.ds(base, PITCH // 2, stride=2), :]
            south = turned[pl.ds(base + 1, PITCH // 2, stride=2), :]
            joined = jnp.concatenate([north[:, 0:waves], south[:, 0:waves]], axis=1)
            plane[pl.ds(part_at, PITCH // 2, stride=2), 0 : 2 * waves] = joined
        spectra_out[s] = jnp.dot(
            plane[0:CHANNELS, 0 : 2 * waves].astype(BF16), weights[s], preferred_element_type=F32
        ).astype(BF16)

    def sent_a(k, carry):
        copy_a(lax.rem(lev + k, levs)).wait_send()
        return carry

    lax.fori_loop(1, levs, sent_a, 0)

    def sent_b(k, carry):
        row, target, here = place_b(k)

        @pl.when(jnp.logical_not(here))
        def _():
            copy_b(row, target).wait_send()

        return carry

    lax.fori_loop(0, waves, sent_b, 0)

    def sent_c(k, carry):
        copy_c(k).wait_send()
        return carry

    lax.fori_loop(1, waves, sent_c, 0)


def body(waves, levs, spectra, vertical, legendre, tile_mask, assign, row_points, quadrature, forcing):
    slots, fields, levels, parts, degrees = spectra.shape
    points = forcing.shape[-1]
    own_rows = waves // levs
    part = own_rows * ROWS
    total_rows = waves * ROWS
    smem = pl.BlockSpec(memory_space=pltpu.SMEM)
    vmem = pl.BlockSpec(memory_space=pltpu.VMEM)
    turned_rows = max(levs, ROWS) * LANES
    grid, spectra_out = pl.pallas_call(
        functools.partial(kernel, waves, levs),
        out_shape=(
            jax.ShapeDtypeStruct((CHANNELS, points), BF16),
            jax.ShapeDtypeStruct((slots, CHANNELS, degrees), BF16),
        ),
        in_specs=[vmem, vmem, smem, smem, smem, smem, vmem, vmem],
        out_specs=(vmem, vmem),
        scratch_shapes=[
            pltpu.VMEM((slots, 2 * waves, degrees), BF16),
            pltpu.VMEM((levs * LEVEL_PITCH, levs * LEVEL_PITCH), BF16),
            pltpu.VMEM((THIRDS * total_rows, points), BF16),
            pltpu.VMEM((LANES, LANES), F32),
            pltpu.VMEM((levs * LANES + 8, LANES), F32),
            pltpu.VMEM((turned_rows, LANES), F32),
            pltpu.VMEM((total_rows + 8, LANES), F32),
            pltpu.VMEM((PITCH, THIRDS * total_rows), BF16),
            pltpu.VMEM((CHANNELS, points), BF16),
            pltpu.VMEM((total_rows, LANES), BF16),
            pltpu.VMEM((levs, part, LANES), BF16),
            pltpu.VMEM((levs, own_rows, ROWS, LANES), BF16),
            pltpu.VMEM((waves, ROWS, LANES), BF16),
            pltpu.VMEM((waves, ROWS, LANES), BF16),
            pltpu.VMEM((waves, ROWS, LANES), BF16),
            pltpu.SemaphoreType.DMA((3,)),
            pltpu.SemaphoreType.DMA((3,)),
        ],
        compiler_params=pltpu.CompilerParams(
            collective_id=0, has_side_effects=True, vmem_limit_bytes=56 * 1024 * 1024
        ),
    )(
        spectra.reshape(slots, CHANNELS, degrees),
        legendre,
        tile_mask.reshape(slots, tile_mask.shape[1]),
        assign,
        row_points,
        quadrature,
        vertical,
        forcing.reshape(CHANNELS, points),
    )
    return grid.reshape(forcing.shape), spectra_out.reshape(spectra.shape)


def solution(mesh):
    return jax.shard_map(
        functools.partial(body, mesh.shape["wave"], mesh.shape["lev"]),
        mesh=mesh,
        in_specs=(
            P("wave", None, "lev", None, None),
            P(),
            P("wave", None, None),
            P("wave", None, None),
            P(),
            P("wave"),
            P("wave"),
            P(None, "lev", None, "wave", None),
        ),
        out_specs=(P(None, "lev", None, "wave", None), P("wave", None, "lev", None, None)),
        check_vma=False,
    )
```

time: 200 us -> 68.8 us (0.34)
  other arithmetic: 97.3 us -> 0 us
  Pallas kernels: 0 us -> 57.4 us
  starting transfers between devices: 28.8 us -> 0 us
  waiting for transfers between devices: 21.3 us -> 0 us
  between operations: 15.7 us -> 1.93 us
  matrix products: 13.1 us -> 0 us
  local copies, waits for them, and re-layouts: 21.5 us -> 9.09 us
    convert_element_type x3 -> x0, other arithmetic: 95.6 us -> none  [the longest x1 95.6 us: phase_table(): jnp.where(usable, jnp.cos(angles), jnp.float32(0.0)).astype(jnp.bfloat16)]
    pallas_call x0 -> x1, Pallas kernels: none -> 57.4 us  [body(): pl.pallas_call(functools.partial(kernel, waves, levs), out_shape=(jax.Sha...]
    all_to_all x2 -> x0, starting transfers between devices: 28.8 us -> none  [the longest x1 24.1 us: body(): lax.all_to_all(fourier, 'wave', split_axis=0, concat_axis=5, tiled=True)]
    all_to_all x2 -> x0, waiting for transfers between devices: 21.3 us -> none  [the longest x1 10.9 us: body(): lax.all_to_all(fourier, 'wave', split_axis=0, concat_axis=5, tiled=True)]
    dot_general x5 -> x0, matrix products: 13.1 us -> none  [the longest x1 4.46 us: row_dense(): jnp.dot(channel_rows, phase_rows, preferred_element_type=jnp.float32)]
    unnamed x18 -> x1, local copies, waits for them, and re-layouts: 10.2 us -> 1.29 us
    reshape x0 -> x4, local copies, waits for them, and re-layouts: none -> 7.8 us  [the longest x2 3.93 us: body(): return (grid.reshape(forcing.shape), spectra_out.reshape(spectra.shape))]
    another operation x3 -> x0, local copies, waits for them, and re-layouts: 3.59 us -> none  [the longest x2 2.71 us: body(): weighted_all = jnp.stack(weighted_rows, 0)]
  transfers between devices with their start and end apart: 3 -> 0, of which waited for: 2 -> 0; matrix products, arithmetic and copies ran while one was open for 50% -> 0% of each run, Pallas kernels for 0% -> 0%
where the time goes in v1:
time: 68.8 us; the launch traced here: 68.4 us
  Pallas kernels  57.4 us (83%)
  local copies, waits for them, and re-layouts  9.09 us (13%)
  between operations  1.93 us (3%)
    pallas_call x1, Pallas kernels, body(): pl.pallas_call(functools.partial(kernel, waves, levs), out_shape=(jax.Sha...  57.4 us
    reshape x2, local copies, waits for them, and re-layouts, body(): return (grid.reshape(forcing.shape), spectra_out.reshape(spectra.shape))  3.93 us
    reshape x1, local copies, waits for them, and re-layouts, body(): spectra.reshape(slots, CHANNELS, degrees)  1.98 us
    reshape x1, local copies, waits for them, and re-layouts, body(): forcing.reshape(CHANNELS, points)  1.89 us

profile of v1, /device:TPU:1, one launch (start us, length us, event | category | flops | bytes accessed | tf_op | source)
XLA Modules:
  0.0 68.4 jit_solution(8296470616895557507)
XLA Ops:
  1.9 1.3 %copy.13 = s32[10,10,1]{1,0,2:T(8,128)} copy(s32[10,10,1]{1,2,0:T(1,128)} %param.11) | data formatting | bytes 800
  3.2 1.9 %reshape.21.forcing = bf16[36,2688]{1,0:T(8,128)(2,1)} reshape(bf16[3,6,2,1,2688]{4,2,3,1,0:T(2,128)(2,1)} %param.15) | data formatting | bytes 387072 | tf_op jit(solution)/shard_map/reshape | solution.py:419
  5.1 2.0 %reshape.19.spectra = bf16[10,36,640]{2,1,0:T(8,128)(2,1)} reshape(bf16[10,3,6,2,640]{4,3,2,1,0:T(2,128)(2,1)} %param.8) | data formatting | bytes 921600 | tf_op jit(solution)/shard_map/reshape | solution.py:412
  7.1 57.4 %shard_map.95 = (bf16[36,2688]{1,0:T(8,128)(2,1)}, bf16[10,36,640]{2,1,0:T(8,128)(2,1)}) custom-call(bf16[10,36,640]{2,1,0:T(8,128)(2,1)} %reshape.19.spectra, bf16[10,64,640]{2,1,0:T(8,128)(2,1)} %legendre.1, s32[10,10]{1,0:T(8,128)} %bitcast.7, s32[640]{0:T(1024)} %assign.1, s32[1]{0:T(128)S(6)} %copy.14.row_points, f32[1]{0:T(128)S(6)} %copy.15.quadrature, ...), custom_call_target="tpu_custom_call" | custom-call | tf_op jit(solution)/shard_map/pallas_call | solution.py:381
  64.5 1.8 %reshape.22 = bf16[3,6,2,1,2688]{4,2,1,0,3:T(2,128)(2,1)} reshape(bf16[36,2688]{1,0:T(8,128)(2,1)} %get-tuple-element.4) | data formatting | bytes 387072 | tf_op jit(solution)/shard_map/reshape | solution.py:421
  66.3 2.1 %reshape.23 = bf16[10,3,6,2,640]{4,3,2,1,0:T(2,128)(2,1)} reshape(bf16[10,36,640]{2,1,0:T(8,128)(2,1)} %get-tuple-element.5) | data formatting | bytes 921600 | tf_op jit(solution)/shard_map/reshape | solution.py:421

commit v2 on v1

--- a/solution.py
+++ b/solution.py
@@ -21,20 +21,49 @@
 LEVEL_PITCH = 24
 ROWS = 2 * GROUPS
 CHANNELS = 2 * FIELDS * OWN_LEVELS
+STEP_WAVES = 4
+RING = 8
 NT_DIMS = (((1,), (1,)), ((), ()))
 
 
 def cosine_of_turns(turns):
-    angle = (turns - jnp.round(turns)) * F32(2.0 * math.pi)
-    square = angle * angle
-    total = jnp.full_like(square, (-1.0) ** 9 / math.factorial(18))
-    for k in range(8, -1, -1):
-        total = total * square + F32((-1.0) ** k / math.factorial(2 * k))
+    reduced = turns - jnp.round(turns)
+    square = reduced * reduced
+    terms = [(-1.0) ** k * (2.0 * math.pi) ** (2 * k) / math.factorial(2 * k) for k in range(9)]
+    total = square * F32(terms[8]) + F32(terms[7])
+    for term in terms[6::-1]:
+        total = total * square + F32(term)
     return total
 
 
 def turns_of(product, length, inverse):
     return (product - jnp.floor(product * inverse) * length) * inverse
+
+
+def low(value, size):
+    return value & (size - 1)
+
+
+def high(value, size):
+    return value >> (size.bit_length() - 1)
+
+
+def far_first(index, size):
+    step = (index + 1) >> 1
+    return low(size // 2 + jnp.where((index & 1) == 0, step, -step), size)
+
+
+def wave_partner(index, wave, waves):
+    rows = waves // RING
+    up = low(high(wave, RING) + far_first(high(index, RING), rows), rows)
+    side = low(wave + far_first(low(index, RING), RING), RING)
+    return up * RING + side
+
+
+def lev_partner(index, lev, levs):
+    chips = levs // 2
+    chip = low((lev >> 1) + far_first(index >> 1, chips), chips)
+    return chip * 2 + ((lev + index + 1) & 1)
 
 
 def slots_of():
@@ -69,44 +98,63 @@
     recv_b,
     send_c,
     recv_c,
+    spectra_in,
+    legendre_in,
+    forcing_in,
+    grid_held,
+    spectra_held,
     send_sems,
     recv_sems,
+    load_sems,
+    store_sems,
 ):
     wave = lax.axis_index("wave")
     lev = lax.axis_index("lev")
     own_rows = waves // levs
     part = own_rows * ROWS
     total_rows = waves * ROWS
-    degrees = spectra.shape[2]
-    points = forcing.shape[1]
+    degrees = spectra.shape[3]
+    points = forcing.shape[2]
+    block_waves = LANES // ROWS
+    blocks = waves // block_waves
+
+    loads = []
+    for at, (source, held) in enumerate(((legendre, legendre_in), (spectra, spectra_in))):
+        load = pltpu.make_async_copy(source, held, load_sems.at[at])
+        load.start()
+        loads.append(load)
+    load_forcing = pltpu.make_async_copy(forcing, forcing_in, load_sems.at[2])
+    load_forcing.start()
 
     barrier = pltpu.get_barrier_semaphore()
+
+    def greet_wave(k, carry):
+        pl.semaphore_signal(
+            barrier, inc=1, device_id=(wave_partner(k, wave, waves), lev), device_id_type=MESH
+        )
+        return carry
 
     def greet_lev(k, carry):
         pl.semaphore_signal(
-            barrier, inc=1, device_id=(wave, lax.rem(lev + k, levs)), device_id_type=MESH
-        )
-        return carry
-
-    def greet_wave(k, carry):
-        pl.semaphore_signal(
-            barrier, inc=1, device_id=(lax.rem(wave + k, waves), lev), device_id_type=MESH
-        )
-        return carry
-
-    lax.fori_loop(1, levs, greet_lev, 0)
-    lax.fori_loop(1, waves, greet_wave, 0)
+            barrier, inc=1, device_id=(wave, lev_partner(k, lev, levs)), device_id_type=MESH
+        )
+        return carry
+
+    lax.fori_loop(0, waves - 1, greet_wave, 0)
+    lax.fori_loop(0, levs - 1, greet_lev, 0)
 
     turned[...] = jnp.zeros_like(turned)
     plane[...] = jnp.zeros_like(plane)
     degree = lax.broadcasted_iota(jnp.int32, (1, degrees), 1)
     lane = lax.broadcasted_iota(jnp.int32, (1, LANES), 1)
     half = degrees // (2 * LANES // 2)
+    for load in loads:
+        load.wait()
     for s, third, group in slots_of():
         wave_number = assign[wave * SLOTS + s]
         marks = jnp.concatenate(
             [
-                jnp.where(lane < LANES // 2, tiles[s, 2 * k], tiles[s, 2 * k + 1])
+                jnp.where(lane < LANES // 2, tiles[s, 0, 2 * k], tiles[s, 0, 2 * k + 1])
                 for k in range(half)
             ],
             axis=1,
@@ -114,13 +162,13 @@
         offset = degree - wave_number
         live = jnp.where((marks > 0) & (offset >= 0), F32(1.0), F32(0.0))
         signed = jnp.where((offset & 1) == 0, live, -live)
-        table = legendre[s].astype(F32)
+        table = legendre_in[s].astype(F32)
         lath = table.shape[0]
         weights[s, 0:lath, :] = (table * live).astype(BF16)
         weights[s, lath : 2 * lath, :] = (table * signed).astype(BF16)
         factor = jnp.where(wave_number == 0, F32(1.0), F32(2.0))
         plane[0:CHANNELS, 0 : 2 * lath] = factor * lax.dot_general(
-            spectra[s], weights[s], NT_DIMS, preferred_element_type=F32
+            spectra_in[s].reshape(CHANNELS, degrees), weights[s], NT_DIMS, preferred_element_type=F32
         )
         for part_at in range(2):
             block = plane[pl.ds(part_at, PITCH // 2, stride=2), :]
@@ -148,10 +196,10 @@
         )
 
     def start_a(k, carry):
-        copy_a(lax.rem(lev + k, levs)).start()
-        return carry
-
-    lax.fori_loop(1, levs, start_a, 0)
+        copy_a(lev_partner(k, lev, levs)).start()
+        return carry
+
+    lax.fori_loop(0, levs - 1, start_a, 0)
     own_a = pltpu.make_async_copy(
         send_a.at[pl.ds(pl.multiple_of(lev * part, part), part), :],
         recv_a.at[lev],
@@ -179,50 +227,50 @@
     length = row_points[0]
     length_f = length.astype(F32)
     inverse = F32(1.0) / length_f
-    fine = THIRDS * 2 * ROWS
-    at = lax.broadcasted_iota(jnp.int32, (2 * ROWS, LANES), 0)
+    tall = STEP_WAVES * ROWS
+    at = lax.broadcasted_iota(jnp.int32, (tall, LANES), 0)
     at_pair = at >> 1
-    quarter = (at & 1).astype(F32) * F32(0.25)
-    column = lax.broadcasted_iota(jnp.int32, (2 * ROWS, LANES), 1).astype(F32)
+    odd = jnp.concatenate([(at & 1) == 1] * THIRDS, axis=0)
+    quarters = jnp.where(odd, F32(0.25), F32(0.0))
+    column = lax.broadcasted_iota(jnp.int32, (THIRDS * tall, LANES), 1).astype(F32)
+    group_at = at_pair & (GROUPS - 1)
+    real = jnp.concatenate(
+        [jnp.where(group_at < SLOTS - third * GROUPS, F32(1.0), F32(0.0)) for third in range(THIRDS)],
+        axis=0,
+    )
+    steps = waves // STEP_WAVES
 
     def phase_rows(step, carry):
         numbers = []
         for third in range(THIRDS):
-            number = jnp.zeros((2 * ROWS, LANES), jnp.int32)
-            for pair in range(2):
+            number = jnp.zeros((tall, LANES), jnp.int32)
+            for near in range(STEP_WAVES):
                 for group in range(GROUPS):
                     s = third * GROUPS + group
                     if s < SLOTS:
-                        held = assign[(step * 2 + pair) * SLOTS + s]
-                        number = jnp.where(at_pair == pair * GROUPS + group, held, number)
+                        held = assign[(step * STEP_WAVES + near) * SLOTS + s]
+                        number = jnp.where(at_pair == near * GROUPS + group, held, number)
             numbers.append(number)
         number = jnp.concatenate(numbers, axis=0)
-        real = [[s < SLOTS for s in range(t * GROUPS, (t + 1) * GROUPS)] for t in range(THIRDS)]
-        usable = 2 * number < length
-        group_at = at_pair & (GROUPS - 1)
-        kept = jnp.concatenate(
-            [jnp.where(group_at < sum(real[t]), F32(1.0), F32(0.0)) for t in range(THIRDS)], axis=0
-        )
-        kept = jnp.where(usable, kept, F32(0.0))
+        kept = jnp.where(2 * number < length, real, F32(0.0))
         number = number.astype(F32)
-        columns = jnp.concatenate([column] * THIRDS, axis=0)
-        quarters = jnp.concatenate([quarter] * THIRDS, axis=0)
-        before = kept * cosine_of_turns(turns_of(number * columns, length_f, inverse) + quarters)
+        before = kept * cosine_of_turns(turns_of(number * column, length_f, inverse) + quarters)
         now = kept * cosine_of_turns(
-            turns_of(number * (columns + F32(LANES)), length_f, inverse) + quarters
-        )
-        twice = F32(2.0) * cosine_of_turns(turns_of(number * F32(LANES), length_f, inverse))
+            turns_of(number * (column + F32(LANES)), length_f, inverse) + quarters
+        )
+        first = jnp.broadcast_to(now[:, 0:1], now.shape)
+        twice = F32(2.0) * jnp.where(odd, pltpu.roll(first, 1, axis=0), first)
         for block in range(points // LANES):
             value = before.astype(BF16)
             for third in range(THIRDS):
                 phase[
-                    pl.ds(pl.multiple_of(third * total_rows + step * 2 * ROWS, 2 * ROWS), 2 * ROWS),
+                    pl.ds(pl.multiple_of(third * total_rows + step * tall, tall), tall),
                     block * LANES : (block + 1) * LANES,
-                ] = value[third * 2 * ROWS : (third + 1) * 2 * ROWS, :]
+                ] = value[third * tall : (third + 1) * tall, :]
             before, now = now, twice * now - before
         return carry
 
-    lax.fori_loop(0, waves // 2, phase_rows, 0)
+    lax.fori_loop(0, steps * 3 // 8, phase_rows, 0)
 
     whole_a = pltpu.make_async_copy(recv_a, recv_a, recv_sems.at[0])
     whole_a.wait()
@@ -248,9 +296,8 @@
         send_b[target] = flipped.astype(BF16).reshape(own_rows, ROWS, LANES)
 
     def place_b(k):
-        turn = lax.rem(k + wave + lev, waves)
-        target = turn // own_rows
-        row = lax.rem(turn, own_rows)
+        target = lev_partner(high(k, own_rows), lev, levs)
+        row = low(k, own_rows)
         return row, target, (lev * own_rows + row == wave) & (target == lev)
 
     def copy_b(row, target):
@@ -268,7 +315,9 @@
 
         @pl.when(here)
         def _():
-            pltpu.make_async_copy(send_b.at[target, row], recv_b.at[wave], recv_sems.at[1]).start()
+            pltpu.make_async_copy(
+                send_b.at[target, row], recv_b.at[wave], recv_sems.at[1]
+            ).start()
 
         @pl.when(jnp.logical_not(here))
         def _():
@@ -277,41 +326,35 @@
         return carry
 
     lax.fori_loop(0, waves, start_b, 0)
+    lax.fori_loop(steps * 3 // 8, steps, phase_rows, 0)
+
+    load_forcing.wait()
+    chunk = 3 * LANES if points % (3 * LANES) == 0 else LANES
     pltpu.make_async_copy(recv_b, recv_b, recv_sems.at[1]).wait()
-
     received = recv_b[...].astype(F32).reshape(total_rows, LANES)
-    for block in range(total_rows // LANES):
+    for block in range(blocks):
         flipped = received[block * LANES : (block + 1) * LANES, :].T
         for third in range(THIRDS):
             at_lane = third * total_rows + block * LANES
             channels[:, at_lane : at_lane + LANES] = flipped[
                 third * PITCH : (third + 1) * PITCH, :
             ].astype(BF16)
-    chunk = 3 * LANES if points % (3 * LANES) == 0 else LANES
     for first in range(0, points, chunk):
         inside = first + lax.broadcasted_iota(jnp.int32, (CHANNELS, chunk), 1) < length
         grid = jnp.dot(
             channels[0:CHANNELS, :], phase[:, first : first + chunk], preferred_element_type=F32
         )
         grid = jnp.where(inside, grid, F32(0.0)).astype(BF16)
-        grid_out[:, first : first + chunk] = grid
-        both = grid.astype(F32) + forcing[:, first : first + chunk].astype(F32)
-        summed[:, first : first + chunk] = jnp.where(inside, both, F32(0.0)).astype(BF16)
+        grid_held[:, :, first : first + chunk] = grid.reshape(CHANNELS // 2, 2, chunk)
+        added = forcing_in[:, :, first : first + chunk].reshape(CHANNELS, chunk).astype(F32)
+        both = jnp.where(inside, grid.astype(F32) + added, F32(0.0))
+        summed[:, first : first + chunk] = both.astype(BF16)
+    store_grid = pltpu.make_async_copy(grid_held, grid_out, store_sems.at[0])
+    store_grid.start()
     scale = quadrature[0] / length_f
     plane[...] = jnp.zeros_like(plane)
-    for block in range(total_rows // LANES):
-        for third in range(THIRDS):
-            first = third * total_rows + block * LANES
-            back = lax.dot_general(
-                summed[...], phase[first : first + LANES, :], NT_DIMS, preferred_element_type=F32
-            )
-            plane[third * PITCH : third * PITCH + CHANNELS, :] = back * scale
-        send_c[block * LANES // ROWS : (block + 1) * LANES // ROWS] = (
-            plane[...].T.astype(BF16).reshape(LANES // ROWS, ROWS, LANES)
-        )
-
-    def copy_c(k):
-        target = lax.rem(wave + k, waves)
+
+    def copy_c(target):
         return pltpu.make_async_remote_copy(
             src_ref=send_c.at[target],
             dst_ref=recv_c.at[wave],
@@ -321,11 +364,22 @@
             device_id_type=MESH,
         )
 
+    for block in range(blocks):
+        for third in range(THIRDS):
+            first = third * total_rows + block * LANES
+            back = lax.dot_general(
+                summed[...], phase[first : first + LANES, :], NT_DIMS, preferred_element_type=F32
+            )
+            plane[third * PITCH : third * PITCH + CHANNELS, :] = back * scale
+        send_c[block * block_waves : (block + 1) * block_waves] = (
+            plane[...].T.astype(BF16).reshape(block_waves, ROWS, LANES)
+        )
+
     def start_c(k, carry):
-        copy_c(k).start()
-        return carry
-
-    lax.fori_loop(1, waves, start_c, 0)
+        copy_c(wave_partner(k, wave, waves)).start()
+        return carry
+
+    lax.fori_loop(0, waves - 1, start_c, 0)
     pltpu.make_async_copy(send_c.at[wave], recv_c.at[wave], recv_sems.at[2]).start()
     pltpu.make_async_copy(recv_c, recv_c, recv_sems.at[2]).wait()
 
@@ -341,15 +395,17 @@
             south = turned[pl.ds(base + 1, PITCH // 2, stride=2), :]
             joined = jnp.concatenate([north[:, 0:waves], south[:, 0:waves]], axis=1)
             plane[pl.ds(part_at, PITCH // 2, stride=2), 0 : 2 * waves] = joined
-        spectra_out[s] = jnp.dot(
+        spectra_held[s] = jnp.dot(
             plane[0:CHANNELS, 0 : 2 * waves].astype(BF16), weights[s], preferred_element_type=F32
-        ).astype(BF16)
+        ).astype(BF16).reshape(CHANNELS // 2, 2, degrees)
+    store_spectra = pltpu.make_async_copy(spectra_held, spectra_out, store_sems.at[1])
+    store_spectra.start()
 
     def sent_a(k, carry):
-        copy_a(lax.rem(lev + k, levs)).wait_send()
-        return carry
-
-    lax.fori_loop(1, levs, sent_a, 0)
+        copy_a(lev_partner(k, lev, levs)).wait_send()
+        return carry
+
+    lax.fori_loop(0, levs - 1, sent_a, 0)
 
     def sent_b(k, carry):
         row, target, here = place_b(k)
@@ -363,10 +419,12 @@
     lax.fori_loop(0, waves, sent_b, 0)
 
     def sent_c(k, carry):
-        copy_c(k).wait_send()
+        copy_c(low(wave + k, waves)).wait_send()
         return carry
 
     lax.fori_loop(1, waves, sent_c, 0)
+    store_spectra.wait()
+    store_grid.wait()
 
 
 def body(waves, levs, spectra, vertical, legendre, tile_mask, assign, row_points, quadrature, forcing):
@@ -377,15 +435,16 @@
     total_rows = waves * ROWS
     smem = pl.BlockSpec(memory_space=pltpu.SMEM)
     vmem = pl.BlockSpec(memory_space=pltpu.VMEM)
+    hbm = pl.BlockSpec(memory_space=pl.ANY)
     turned_rows = max(levs, ROWS) * LANES
     grid, spectra_out = pl.pallas_call(
         functools.partial(kernel, waves, levs),
         out_shape=(
-            jax.ShapeDtypeStruct((CHANNELS, points), BF16),
-            jax.ShapeDtypeStruct((slots, CHANNELS, degrees), BF16),
+            jax.ShapeDtypeStruct((CHANNELS // 2, 2, points), BF16),
+            jax.ShapeDtypeStruct((slots, CHANNELS // 2, 2, degrees), BF16),
         ),
-        in_specs=[vmem, vmem, smem, smem, smem, smem, vmem, vmem],
-        out_specs=(vmem, vmem),
+        in_specs=[hbm, hbm, smem, smem, smem, smem, vmem, hbm],
+        out_specs=(hbm, hbm),
         scratch_shapes=[
             pltpu.VMEM((slots, 2 * waves, degrees), BF16),
             pltpu.VMEM((levs * LEVEL_PITCH, levs * LEVEL_PITCH), BF16),
@@ -402,21 +461,28 @@
             pltpu.VMEM((waves, ROWS, LANES), BF16),
             pltpu.VMEM((waves, ROWS, LANES), BF16),
             pltpu.VMEM((waves, ROWS, LANES), BF16),
+            pltpu.VMEM((slots, CHANNELS // 2, 2, degrees), BF16),
+            pltpu.VMEM(legendre.shape, BF16),
+            pltpu.VMEM((CHANNELS // 2, 2, points), BF16),
+            pltpu.VMEM((CHANNELS // 2, 2, points), BF16),
+            pltpu.VMEM((slots, CHANNELS // 2, 2, degrees), BF16),
             pltpu.SemaphoreType.DMA((3,)),
             pltpu.SemaphoreType.DMA((3,)),
+            pltpu.SemaphoreType.DMA((3,)),
+            pltpu.SemaphoreType.DMA((2,)),
         ],
         compiler_params=pltpu.CompilerParams(
             collective_id=0, has_side_effects=True, vmem_limit_bytes=56 * 1024 * 1024
         ),
     )(
-        spectra.reshape(slots, CHANNELS, degrees),
+        spectra.reshape(slots, CHANNELS // 2, 2, degrees),
         legendre,
-        tile_mask.reshape(slots, tile_mask.shape[1]),
+        jnp.transpose(tile_mask, (0, 2, 1)),
         assign,
         row_points,
         quadrature,
         vertical,
-        forcing.reshape(CHANNELS, points),
+        forcing.reshape(CHANNELS // 2, 2, points),
     )
     return grid.reshape(forcing.shape), spectra_out.reshape(spectra.shape)
 

time: 68.8 us -> 60.4 us (0.88)
  local copies, waits for them, and re-layouts: 9.09 us -> 3.84 us
  Pallas kernels: 57.4 us -> 54.3 us
    reshape x4 -> x0, local copies, waits for them, and re-layouts: 7.8 us -> none  [the longest x2 3.93 us: body(): return (grid.reshape(forcing.shape), spectra_out.reshape(spectra.shape))]
    pallas_call x1, Pallas kernels: 57.4 us -> 54.3 us  [body(): pl.pallas_call(functools.partial(kernel, waves, levs), out_shape=(jax.Sha...]
    unnamed x1 -> x2, local copies, waits for them, and re-layouts: 1.29 us -> 3.84 us
where the time goes in v2:
time: 60.4 us; the launch traced here: 60.1 us
  Pallas kernels  54.3 us (90%)
  local copies, waits for them, and re-layouts  3.84 us (6%)
  between operations  1.93 us (3%)
    pallas_call x1, Pallas kernels, body(): pl.pallas_call(functools.partial(kernel, waves, levs), out_shape=(jax.Sha...  54.3 us
    unnamed x2, local copies, waits for them, and re-layouts  3.84 us

profile of v2, /device:TPU:1, one launch (start us, length us, event | category | flops | bytes accessed | tf_op | source)
XLA Modules:
  0.0 60.1 jit_solution(17710833693328237225)
XLA Ops:
  1.9 54.3 %shard_map.95 = (bf16[18,2,2688]{2,1,0:T(2,128)(2,1)}, bf16[10,18,2,640]{3,2,1,0:T(2,128)(2,1)}) custom-call(bf16[10,18,2,640]{3,2,1,0:T(2,128)(2,1)} %bitcast.8, bf16[10,64,640]{2,1,0:T(8,128)(2,1)} %legendre.1, s32[10,1,10]{2,1,0:T(1,128)} %bitcast.11, s32[640]{0:T(1024)} %assign.1, s32[1]{0:T(128)S(6)} %copy.13.row_points, f32[1]{0:T(128)S(6)} %copy.14.quadrature, ...), custom_call_target="tpu_custom_call" | custom-call | tf_op jit(solution)/shard_map/pallas_call | solution.py:440
  56.2 1.7 %copy.15 = bf16[3,6,2,1,2688]{4,2,3,1,0:T(2,128)(2,1)} copy(bf16[3,6,2,1,2688]{4,2,3,1,0:T(2,128)(2,1)} %bitcast.10) | data formatting | bytes 387072
  58.0 2.1 %copy.16 = bf16[10,3,6,2,640]{4,3,2,1,0:T(2,128)(2,1)} copy(bf16[10,3,6,2,640]{4,3,2,1,0:T(2,128)(2,1)} %bitcast.7) | data formatting | bytes 921600

commit v3 on v2

--- a/solution.py
+++ b/solution.py
@@ -22,6 +22,7 @@
 ROWS = 2 * GROUPS
 CHANNELS = 2 * FIELDS * OWN_LEVELS
 STEP_WAVES = 4
+VMEM_BYTES = 56 * 1024 * 1024
 RING = 8
 NT_DIMS = (((1,), (1,)), ((), ()))
 
@@ -101,6 +102,11 @@
     spectra_in,
     legendre_in,
     forcing_in,
+    vertical_in,
+    tiles_in,
+    assign_in,
+    row_points_in,
+    quadrature_in,
     grid_held,
     spectra_held,
     send_sems,
@@ -118,13 +124,22 @@
     block_waves = LANES // ROWS
     blocks = waves // block_waves
 
-    loads = []
-    for at, (source, held) in enumerate(((legendre, legendre_in), (spectra, spectra_in))):
-        load = pltpu.make_async_copy(source, held, load_sems.at[at])
+    pairs = (
+        (assign, assign_in),
+        (tiles, tiles_in),
+        (legendre, legendre_in),
+        (spectra, spectra_in),
+        (vertical, vertical_in),
+        (row_points, row_points_in),
+        (quadrature, quadrature_in),
+        (forcing, forcing_in),
+    )
+    loads = [
+        pltpu.make_async_copy(source, held, load_sems.at[at])
+        for at, (source, held) in enumerate(pairs)
+    ]
+    for load in loads:
         load.start()
-        loads.append(load)
-    load_forcing = pltpu.make_async_copy(forcing, forcing_in, load_sems.at[2])
-    load_forcing.start()
 
     barrier = pltpu.get_barrier_semaphore()
 
@@ -151,10 +166,10 @@
     for load in loads:
         load.wait()
     for s, third, group in slots_of():
-        wave_number = assign[wave * SLOTS + s]
+        wave_number = assign_in[wave * SLOTS + s]
         marks = jnp.concatenate(
             [
-                jnp.where(lane < LANES // 2, tiles[s, 0, 2 * k], tiles[s, 0, 2 * k + 1])
+                jnp.where(lane < LANES // 2, tiles_in[s, 0, 2 * k], tiles_in[s, 0, 2 * k + 1])
                 for k in range(half)
             ],
             axis=1,
@@ -183,31 +198,7 @@
         spread[pl.ds(row, waves, stride=ROWS), :] = flipped[0:waves, :]
     send_a[...] = spread[0:total_rows, :].astype(BF16)
 
-    pl.semaphore_wait(barrier, levs - 1 + waves - 1)
-
-    def copy_a(target):
-        return pltpu.make_async_remote_copy(
-            src_ref=send_a.at[pl.ds(pl.multiple_of(target * part, part), part), :],
-            dst_ref=recv_a.at[lev],
-            send_sem=send_sems.at[0],
-            recv_sem=recv_sems.at[0],
-            device_id=(wave, target),
-            device_id_type=MESH,
-        )
-
-    def start_a(k, carry):
-        copy_a(lev_partner(k, lev, levs)).start()
-        return carry
-
-    lax.fori_loop(0, levs - 1, start_a, 0)
-    own_a = pltpu.make_async_copy(
-        send_a.at[pl.ds(pl.multiple_of(lev * part, part), part), :],
-        recv_a.at[lev],
-        recv_sems.at[0],
-    )
-    own_a.start()
-
-    levels = vertical.shape[1]
+    levels = vertical_in.shape[1]
     edge = levs * LEVEL_PITCH
     at_row = lax.broadcasted_iota(jnp.int32, (edge, levels), 0)
     at_level = lax.broadcasted_iota(jnp.int32, (edge, levels), 1)
@@ -220,11 +211,35 @@
         pick = jnp.where((at_field == field) & (at_level == wanted), F32(1.0), F32(0.0)).astype(
             BF16
         )
-        rows = jnp.dot(pick, vertical[field], preferred_element_type=F32).astype(BF16)
+        rows = jnp.dot(pick, vertical_in[field], preferred_element_type=F32).astype(BF16)
         mixed = mixed + lax.dot_general(rows, pick, NT_DIMS, preferred_element_type=F32)
     mixer[...] = mixed.astype(BF16)
 
-    length = row_points[0]
+    pl.semaphore_wait(barrier, levs - 1 + waves - 1)
+
+    def copy_a(target):
+        return pltpu.make_async_remote_copy(
+            src_ref=send_a.at[pl.ds(pl.multiple_of(target * part, part), part), :],
+            dst_ref=recv_a.at[lev],
+            send_sem=send_sems.at[0],
+            recv_sem=recv_sems.at[0],
+            device_id=(wave, target),
+            device_id_type=MESH,
+        )
+
+    def start_a(k, carry):
+        copy_a(lev_partner(k, lev, levs)).start()
+        return carry
+
+    lax.fori_loop(0, levs - 1, start_a, 0)
+    own_a = pltpu.make_async_copy(
+        send_a.at[pl.ds(pl.multiple_of(lev * part, part), part), :],
+        recv_a.at[lev],
+        recv_sems.at[0],
+    )
+    own_a.start()
+
+    length = row_points_in[0]
     length_f = length.astype(F32)
     inverse = F32(1.0) / length_f
     tall = STEP_WAVES * ROWS
@@ -248,7 +263,7 @@
                 for group in range(GROUPS):
                     s = third * GROUPS + group
                     if s < SLOTS:
-                        held = assign[(step * STEP_WAVES + near) * SLOTS + s]
+                        held = assign_in[(step * STEP_WAVES + near) * SLOTS + s]
                         number = jnp.where(at_pair == near * GROUPS + group, held, number)
             numbers.append(number)
         number = jnp.concatenate(numbers, axis=0)
@@ -328,7 +343,6 @@
     lax.fori_loop(0, waves, start_b, 0)
     lax.fori_loop(steps * 3 // 8, steps, phase_rows, 0)
 
-    load_forcing.wait()
     chunk = 3 * LANES if points % (3 * LANES) == 0 else LANES
     pltpu.make_async_copy(recv_b, recv_b, recv_sems.at[1]).wait()
     received = recv_b[...].astype(F32).reshape(total_rows, LANES)
@@ -351,7 +365,7 @@
         summed[:, first : first + chunk] = both.astype(BF16)
     store_grid = pltpu.make_async_copy(grid_held, grid_out, store_sems.at[0])
     store_grid.start()
-    scale = quadrature[0] / length_f
+    scale = quadrature_in[0] / length_f
     plane[...] = jnp.zeros_like(plane)
 
     def copy_c(target):
@@ -381,6 +395,23 @@
 
     lax.fori_loop(0, waves - 1, start_c, 0)
     pltpu.make_async_copy(send_c.at[wave], recv_c.at[wave], recv_sems.at[2]).start()
+    sent_a = send_a.at[pl.ds(0, (levs - 1) * part), :]
+    pltpu.make_async_copy(sent_a, sent_a, send_sems.at[0]).wait()
+    own_among = high(wave, own_rows) == lev
+
+    def wait_sent(held, count, sem):
+        sent = held.at[pl.ds(0, count)]
+        pltpu.make_async_copy(sent, sent, sem).wait()
+
+    @pl.when(own_among)
+    def _():
+        wait_sent(recv_b, waves - 1, send_sems.at[1])
+
+    @pl.when(jnp.logical_not(own_among))
+    def _():
+        wait_sent(recv_b, waves, send_sems.at[1])
+
+    wait_sent(send_c, waves - 1, send_sems.at[2])
     pltpu.make_async_copy(recv_c, recv_c, recv_sems.at[2]).wait()
 
     spread[0:total_rows, :] = recv_c[...].astype(F32).reshape(total_rows, LANES)
@@ -401,30 +432,26 @@
     store_spectra = pltpu.make_async_copy(spectra_held, spectra_out, store_sems.at[1])
     store_spectra.start()
 
-    def sent_a(k, carry):
-        copy_a(lev_partner(k, lev, levs)).wait_send()
-        return carry
-
-    lax.fori_loop(0, levs - 1, sent_a, 0)
-
-    def sent_b(k, carry):
-        row, target, here = place_b(k)
-
-        @pl.when(jnp.logical_not(here))
-        def _():
-            copy_b(row, target).wait_send()
-
-        return carry
-
-    lax.fori_loop(0, waves, sent_b, 0)
-
-    def sent_c(k, carry):
-        copy_c(low(wave + k, waves)).wait_send()
-        return carry
-
-    lax.fori_loop(1, waves, sent_c, 0)
     store_spectra.wait()
     store_grid.wait()
+
+
+def hand_out(grid, spectra, grid_out, spectra_out, grid_held, spectra_held, sems):
+    loads = [
+        pltpu.make_async_copy(spectra, spectra_held, sems.at[0]),
+        pltpu.make_async_copy(grid, grid_held, sems.at[1]),
+    ]
+    stores = [
+        pltpu.make_async_copy(spectra_held, spectra_out, sems.at[2]),
+        pltpu.make_async_copy(grid_held, grid_out, sems.at[3]),
+    ]
+    for load in loads:
+        load.start()
+    for load, store in zip(loads, stores):
+        load.wait()
+        store.start()
+    for store in stores:
+        store.wait()
 
 
 def body(waves, levs, spectra, vertical, legendre, tile_mask, assign, row_points, quadrature, forcing):
@@ -433,8 +460,6 @@
     own_rows = waves // levs
     part = own_rows * ROWS
     total_rows = waves * ROWS
-    smem = pl.BlockSpec(memory_space=pltpu.SMEM)
-    vmem = pl.BlockSpec(memory_space=pltpu.VMEM)
     hbm = pl.BlockSpec(memory_space=pl.ANY)
     turned_rows = max(levs, ROWS) * LANES
     grid, spectra_out = pl.pallas_call(
@@ -443,7 +468,7 @@
             jax.ShapeDtypeStruct((CHANNELS // 2, 2, points), BF16),
             jax.ShapeDtypeStruct((slots, CHANNELS // 2, 2, degrees), BF16),
         ),
-        in_specs=[hbm, hbm, smem, smem, smem, smem, vmem, hbm],
+        in_specs=[hbm] * 8,
         out_specs=(hbm, hbm),
         scratch_shapes=[
             pltpu.VMEM((slots, 2 * waves, degrees), BF16),
@@ -464,15 +489,20 @@
             pltpu.VMEM((slots, CHANNELS // 2, 2, degrees), BF16),
             pltpu.VMEM(legendre.shape, BF16),
             pltpu.VMEM((CHANNELS // 2, 2, points), BF16),
+            pltpu.VMEM(vertical.shape, BF16),
+            pltpu.SMEM((slots, 1, tile_mask.shape[1]), jnp.int32),
+            pltpu.SMEM(assign.shape, jnp.int32),
+            pltpu.SMEM(row_points.shape, jnp.int32),
+            pltpu.SMEM(quadrature.shape, F32),
             pltpu.VMEM((CHANNELS // 2, 2, points), BF16),
             pltpu.VMEM((slots, CHANNELS // 2, 2, degrees), BF16),
             pltpu.SemaphoreType.DMA((3,)),
             pltpu.SemaphoreType.DMA((3,)),
-            pltpu.SemaphoreType.DMA((3,)),
+            pltpu.SemaphoreType.DMA((8,)),
             pltpu.SemaphoreType.DMA((2,)),
         ],
         compiler_params=pltpu.CompilerParams(
-            collective_id=0, has_side_effects=True, vmem_limit_bytes=56 * 1024 * 1024
+            collective_id=0, has_side_effects=True, vmem_limit_bytes=VMEM_BYTES
         ),
     )(
         spectra.reshape(slots, CHANNELS // 2, 2, degrees),
@@ -484,6 +514,21 @@
         vertical,
         forcing.reshape(CHANNELS // 2, 2, points),
     )
+    grid, spectra_out = pl.pallas_call(
+        hand_out,
+        out_shape=(
+            jax.ShapeDtypeStruct(grid.shape, BF16),
+            jax.ShapeDtypeStruct(spectra_out.shape, BF16),
+        ),
+        in_specs=[hbm, hbm],
+        out_specs=(hbm, hbm),
+        scratch_shapes=[
+            pltpu.VMEM(grid.shape, BF16),
+            pltpu.VMEM(spectra_out.shape, BF16),
+            pltpu.SemaphoreType.DMA((4,)),
+        ],
+        compiler_params=pltpu.CompilerParams(vmem_limit_bytes=VMEM_BYTES),
+    )(grid, spectra_out)
     return grid.reshape(forcing.shape), spectra_out.reshape(spectra.shape)
 
 

time: 60.4 us -> 56.9 us (0.942)
  local copies, waits for them, and re-layouts: 3.84 us -> 0 us
    unnamed x2 -> x0, local copies, waits for them, and re-layouts: 3.84 us -> none
    pallas_call x0 -> x1, Pallas kernels: none -> 1.88 us  [body(): pl.pallas_call(hand_out, out_shape=(jax.ShapeDtypeStruct(grid.shape, BF16...]
    pallas_call x1, Pallas kernels: 54.3 us -> 52.9 us  [body(): pl.pallas_call(functools.partial(kernel, waves, levs), out_shape=(jax.Sha...]
where the time goes in v3:
time: 56.9 us; the launch traced here: 56.7 us
  Pallas kernels  54.8 us (96%)
  between operations  1.93 us (3%)
    pallas_call x1, Pallas kernels, body(): pl.pallas_call(functools.partial(kernel, waves, levs), out_shape=(jax.Sha...  52.9 us
    pallas_call x1, Pallas kernels, body(): pl.pallas_call(hand_out, out_shape=(jax.ShapeDtypeStruct(grid.shape, BF16...  1.88 us

profile of v3, /device:TPU:1, one launch (start us, length us, event | category | flops | bytes accessed | tf_op | source)
XLA Modules:
  0.0 56.7 jit_solution(2688386602384547253)
XLA Ops:
  1.9 52.9 %shard_map.95 = (bf16[18,2,2688]{2,1,0:T(2,128)(2,1)}, bf16[10,18,2,640]{3,2,1,0:T(2,128)(2,1)}) custom-call(bf16[10,18,2,640]{3,2,1,0:T(2,128)(2,1)} %bitcast.7, bf16[10,64,640]{2,1,0:T(8,128)(2,1)} %legendre.1, s32[10,1,10]{2,1,0:T(1,128)} %bitcast.9, s32[640]{0:T(1024)} %assign.1, s32[1]{0:T(128)S(6)} %copy.11.row_points, f32[1]{0:T(128)S(6)} %copy.12.quadrature, ...), custom_call_target="tpu_custom_call" | custom-call | tf_op jit(solution)/shard_map/pallas_call | solution.py:465
  54.8 1.9 %shard_map.96 = (bf16[18,2,2688]{2,1,0:T(2,128)(2,1)}, bf16[10,18,2,640]{3,2,1,0:T(2,128)(2,1)}) custom-call(bf16[18,2,2688]{2,1,0:T(2,128)(2,1)} %get-tuple-element.6.grid, bf16[10,18,2,640]{3,2,1,0:T(2,128)(2,1)} %get-tuple-element.7.spectra), custom_call_target="tpu_custom_call" | custom-call | tf_op jit(solution)/shard_map/pallas_call | solution.py:517

commit v4 on v3

--- a/solution.py
+++ b/solution.py
@@ -113,6 +113,8 @@
     recv_sems,
     load_sems,
     store_sems,
+    line_sem,
+    plane_sem,
 ):
     wave = lax.axis_index("wave")
     lev = lax.axis_index("lev")
@@ -143,20 +145,24 @@
 
     barrier = pltpu.get_barrier_semaphore()
 
-    def greet_wave(k, carry):
-        pl.semaphore_signal(
-            barrier, inc=1, device_id=(wave_partner(k, wave, waves), lev), device_id_type=MESH
-        )
+    core = lev & 1
+    chip = lev >> 1
+    chips = levs // 2
+
+    def greet(row, column):
+        pl.semaphore_signal(barrier, inc=1, device_id=(row, column), device_id_type=MESH)
+
+    def greet_plane(k, carry):
+        greet(wave_partner(k, wave, waves), chip * 2 + 1)
         return carry
 
-    def greet_lev(k, carry):
-        pl.semaphore_signal(
-            barrier, inc=1, device_id=(wave, lev_partner(k, lev, levs)), device_id_type=MESH
-        )
+    def greet_line(k, carry):
+        greet(wave, low(chip + far_first(k, chips), chips) * 2)
         return carry
 
-    lax.fori_loop(0, waves - 1, greet_wave, 0)
-    lax.fori_loop(0, levs - 1, greet_lev, 0)
+    lax.fori_loop(0, waves - 1, greet_plane, 0)
+    lax.fori_loop(0, chips - 1, greet_line, 0)
+    greet(wave, lev + 1 - 2 * core)
 
     turned[...] = jnp.zeros_like(turned)
     plane[...] = jnp.zeros_like(plane)
@@ -215,7 +221,14 @@
         mixed = mixed + lax.dot_general(rows, pick, NT_DIMS, preferred_element_type=F32)
     mixer[...] = mixed.astype(BF16)
 
-    pl.semaphore_wait(barrier, levs - 1 + waves - 1)
+    @pl.when(core == 0)
+    def _():
+        pl.semaphore_wait(barrier, levs - 1)
+        pl.semaphore_signal(line_sem, inc=1, device_id=(wave, lev + 1), device_id_type=MESH)
+
+    @pl.when(core == 1)
+    def _():
+        pl.semaphore_wait(line_sem, 1)
 
     def copy_a(target):
         return pltpu.make_async_remote_copy(
@@ -238,6 +251,21 @@
         recv_sems.at[0],
     )
     own_a.start()
+
+    @pl.when(core == 1)
+    def _():
+        pl.semaphore_wait(barrier, 2 * waves - 1)
+
+        def tell(k, carry):
+            pl.semaphore_signal(
+                plane_sem,
+                inc=1,
+                device_id=(wave, lev_partner(k, lev, levs)),
+                device_id_type=MESH,
+            )
+            return carry
+
+        lax.fori_loop(0, levs - 1, tell, 0)
 
     length = row_points_in[0]
     length_f = length.astype(F32)
@@ -339,6 +367,16 @@
             copy_b(row, target).start()
 
         return carry
+
+    @pl.when(core == 0)
+    def _():
+        pl.semaphore_wait(plane_sem, chips)
+
+    if chips > 1:
+
+        @pl.when(core == 1)
+        def _():
+            pl.semaphore_wait(plane_sem, chips - 1)
 
     lax.fori_loop(0, waves, start_b, 0)
     lax.fori_loop(steps * 3 // 8, steps, phase_rows, 0)
@@ -500,6 +538,8 @@
             pltpu.SemaphoreType.DMA((3,)),
             pltpu.SemaphoreType.DMA((8,)),
             pltpu.SemaphoreType.DMA((2,)),
+            pltpu.SemaphoreType.REGULAR,
+            pltpu.SemaphoreType.REGULAR,
         ],
         compiler_params=pltpu.CompilerParams(
             collective_id=0, has_side_effects=True, vmem_limit_bytes=VMEM_BYTES

time: 56.9 us -> 54.4 us (0.956)
  Pallas kernels: 54.8 us -> 52.2 us
    pallas_call x1, Pallas kernels: 52.9 us -> 50.3 us  [body(): pl.pallas_call(functools.partial(kernel, waves, levs), out_shape=(jax.Sha...]
where the time goes in v4:
time: 54.4 us; the launch traced here: 54.1 us
  Pallas kernels  52.2 us (96%)
  between operations  1.93 us (4%)
    pallas_call x1, Pallas kernels, body(): pl.pallas_call(functools.partial(kernel, waves, levs), out_shape=(jax.Sha...  50.3 us
    pallas_call x1, Pallas kernels, body(): pl.pallas_call(hand_out, out_shape=(jax.ShapeDtypeStruct(grid.shape, BF16...  1.88 us

profile of v4, /device:TPU:1, one launch (start us, length us, event | category | flops | bytes accessed | tf_op | source)
XLA Modules:
  0.0 54.1 jit_solution(14595125432742810041)
XLA Ops:
  1.9 50.3 %shard_map.95 = (bf16[18,2,2688]{2,1,0:T(2,128)(2,1)}, bf16[10,18,2,640]{3,2,1,0:T(2,128)(2,1)}) custom-call(bf16[10,18,2,640]{3,2,1,0:T(2,128)(2,1)} %bitcast.7, bf16[10,64,640]{2,1,0:T(8,128)(2,1)} %legendre.1, s32[10,1,10]{2,1,0:T(1,128)} %bitcast.9, s32[640]{0:T(1024)} %assign.1, s32[1]{0:T(128)S(6)} %copy.11.row_points, f32[1]{0:T(128)S(6)} %copy.12.quadrature, ...), custom_call_target="tpu_custom_call" | custom-call | tf_op jit(solution)/shard_map/pallas_call | solution.py:503
  52.3 1.9 %shard_map.96 = (bf16[18,2,2688]{2,1,0:T(2,128)(2,1)}, bf16[10,18,2,640]{3,2,1,0:T(2,128)(2,1)}) custom-call(bf16[18,2,2688]{2,1,0:T(2,128)(2,1)} %get-tuple-element.6.grid, bf16[10,18,2,640]{3,2,1,0:T(2,128)(2,1)} %get-tuple-element.7.spectra), custom_call_target="tpu_custom_call" | custom-call | tf_op jit(solution)/shard_map/pallas_call | solution.py:557

commit v5 on v4

--- a/solution.py
+++ b/solution.py
@@ -160,9 +160,9 @@
         greet(wave, low(chip + far_first(k, chips), chips) * 2)
         return carry
 
-    lax.fori_loop(0, waves - 1, greet_plane, 0)
     lax.fori_loop(0, chips - 1, greet_line, 0)
     greet(wave, lev + 1 - 2 * core)
+    lax.fori_loop(0, waves - 1, greet_plane, 0)
 
     turned[...] = jnp.zeros_like(turned)
     plane[...] = jnp.zeros_like(plane)
@@ -449,7 +449,6 @@
     def _():
         wait_sent(recv_b, waves, send_sems.at[1])
 
-    wait_sent(send_c, waves - 1, send_sems.at[2])
     pltpu.make_async_copy(recv_c, recv_c, recv_sems.at[2]).wait()
 
     spread[0:total_rows, :] = recv_c[...].astype(F32).reshape(total_rows, LANES)
@@ -470,6 +469,7 @@
     store_spectra = pltpu.make_async_copy(spectra_held, spectra_out, store_sems.at[1])
     store_spectra.start()
 
+    wait_sent(send_c, waves - 1, send_sems.at[2])
     store_spectra.wait()
     store_grid.wait()
 

time: 54.4 us -> 54.3 us (level)
  no operation moved by 1% of the time
where the time goes in v5:
time: 54.3 us; the launch traced here: 54.1 us
  Pallas kernels  52.1 us (96%)
  between operations  1.93 us (4%)
    pallas_call x1, Pallas kernels, body(): pl.pallas_call(functools.partial(kernel, waves, levs), out_shape=(jax.Sha...  50.2 us
    pallas_call x1, Pallas kernels, body(): pl.pallas_call(hand_out, out_shape=(jax.ShapeDtypeStruct(grid.shape, BF16...  1.88 us

profile of v5, /device:TPU:1, one launch (start us, length us, event | category | flops | bytes accessed | tf_op | source)
XLA Modules:
  0.0 54.1 jit_solution(930342176558476618)
XLA Ops:
  1.9 50.2 %shard_map.95 = (bf16[18,2,2688]{2,1,0:T(2,128)(2,1)}, bf16[10,18,2,640]{3,2,1,0:T(2,128)(2,1)}) custom-call(bf16[10,18,2,640]{3,2,1,0:T(2,128)(2,1)} %bitcast.7, bf16[10,64,640]{2,1,0:T(8,128)(2,1)} %legendre.1, s32[10,1,10]{2,1,0:T(1,128)} %bitcast.9, s32[640]{0:T(1024)} %assign.1, s32[1]{0:T(128)S(6)} %copy.11.row_points, f32[1]{0:T(128)S(6)} %copy.12.quadrature, ...), custom_call_target="tpu_custom_call" | custom-call | tf_op jit(solution)/shard_map/pallas_call | solution.py:503
  52.2 1.9 %shard_map.96 = (bf16[18,2,2688]{2,1,0:T(2,128)(2,1)}, bf16[10,18,2,640]{3,2,1,0:T(2,128)(2,1)}) custom-call(bf16[18,2,2688]{2,1,0:T(2,128)(2,1)} %get-tuple-element.6.grid, bf16[10,18,2,640]{3,2,1,0:T(2,128)(2,1)} %get-tuple-element.7.spectra), custom_call_target="tpu_custom_call" | custom-call | tf_op jit(solution)/shard_map/pallas_call | solution.py:557
